TPU v7x, 32 devices: a whole 2x2x4 slice. The times are simulated.
32 devices in a mesh: layer: 8 (over y, x, core), latent: 4 (over z).
Axes of the slice: x: 2, y: 2, z: 4, core: 2. Of those that a mesh axis runs over, the one named last changes fastest.
Arguments:
- layer_input: bfloat16 [8, 1024, 4096], P('layer', None, 'latent'), may hold values from -6 to 6
- enc_weight: bfloat16 [8, 4096, 512], P('layer', None, 'latent'), may hold values from -0.09375 to 0.09375
- enc_bias: float32 [8, 512], P('layer', 'latent'), may hold values from -3 to 3
- dec_weight: bfloat16 [8, 3, 512, 4096], P('layer', None, None, 'latent'), may hold values from -0.5 to 0.5
- block_lists: int32 [8, 16, 2], P('layer'), may hold values from 0 to 3, as said below
- block_counts: int32 [8, 16], P('layer'), may hold values from 1 to 2, as said below
Outputs:
- rebuilt: bfloat16 [8, 1024, 4096], P('layer', None, 'latent')
Inputs may be any that keep to these rules, and one draw needn't show every extreme that they name: `block_lists`: each list holds distinct block ids of one layer. `block_counts`: some entry equals 2 in every draw.
All inputs are finite; a program needn't handle non-finite values.
Results may differ from a plain program's by a relative error of at most 0.0055.
Values may be sent and summed in bfloat16 or wider, within the bound.
No kernel may reach another device: no remote copies, remote signals or barrier semaphores. Data moves between devices by JAX's collectives and lax.ppermute only.
A program may use at most 128 MiB of HBM per device.

v0:
```python
import functools

import jax
import jax.numpy as jnp
from jax import lax
from jax.experimental import pallas as pl
from jax.experimental.pallas import tpu as pltpu
from jax.sharding import PartitionSpec as P

VMEM = pl.BlockSpec(memory_space=pltpu.VMEM)
SMEM = pl.BlockSpec(memory_space=pltpu.SMEM)
ANY = pl.BlockSpec(memory_space=pl.ANY)


def swapped(value, step):
    count = lax.axis_size("latent")
    return lax.ppermute(value, "latent", [(i, i ^ step) for i in range(count)])


def passed_along(value, steps):
    count = lax.axis_size("layer")
    return lax.ppermute(value, "layer", [(i, i + steps) for i in range(count - steps)])


def across_cores(value):
    count = lax.axis_size("layer")
    return lax.ppermute(value, "layer", [(i, i ^ 1) for i in range(count)])


def doubling(parts):
    if parts & (parts - 1):
        raise ValueError("latent axis")
    steps, held = [], [0]
    while len(held) < parts:
        steps.append(parts // (2 * len(held)))
        held = held + [distance ^ steps[-1] for distance in held]
    return steps, held


def fetch_rows_kernel(place_ref, encoder_ref, *refs):
    piece_refs, sems = refs[:-1], refs[-1]
    depth = piece_refs[0].shape[0]
    copies = []
    for step in range(len(piece_refs)):
        first = pl.multiple_of(lax.bitwise_xor(place_ref[0], step) * depth, depth)
        copies.append(pltpu.make_async_copy(encoder_ref.at[pl.ds(first, depth)], piece_refs[step], sems.at[step]))
        copies[-1].start()
    for copy in copies:
        copy.wait()


def fetch_rows(place, encoder, parts):
    depth = encoder.shape[0] // parts
    return pl.pallas_call(
        fetch_rows_kernel,
        out_shape=[jax.ShapeDtypeStruct((depth, encoder.shape[1]), encoder.dtype)] * parts,
        in_specs=[SMEM, ANY],
        out_specs=[ANY] * parts,
        scratch_shapes=[pltpu.SemaphoreType.DMA((parts,))],
        compiler_params=pltpu.CompilerParams(vmem_limit_bytes=60 << 20),
        name="fetch_rows",
    )(place, encoder)


def fetch_kernel(source_ref, out_ref, sem):
    copy = pltpu.make_async_copy(source_ref, out_ref, sem)
    copy.start()
    copy.wait()


def fetch(value):
    return pl.pallas_call(
        fetch_kernel,
        out_shape=jax.ShapeDtypeStruct(value.shape, value.dtype),
        in_specs=[ANY],
        out_specs=VMEM,
        scratch_shapes=[pltpu.SemaphoreType.DMA],
        compiler_params=pltpu.CompilerParams(vmem_limit_bytes=48 << 20),
        name="fetch",
    )(value)


def with_lists(decoder, lists):
    tiles, slots = lists.shape
    ids = jnp.pad(lists.astype(decoder.dtype), ((0, -tiles % 16), (0, decoder.shape[1] - slots)))
    return jnp.concatenate([decoder, ids], axis=0)


def encode_kernel(parts, place_ref, relative_ref, bias_ref, x_ref, *refs):
    weight_refs, refs = refs[:parts], refs[parts:]
    out_refs, partial = refs[:parts], refs[parts]
    width = bias_ref.shape[1]
    tiles, slots, rows, _ = out_refs[0].shape
    pair = 1 + (parts > 1)
    for first in range(0, parts, pair):
        stacked = jnp.concatenate([ref[...] for ref in weight_refs[first : first + pair]], axis=1)
        product = jnp.dot(x_ref[...], stacked, preferred_element_type=jnp.float32)
        for source in range(first, first + pair):
            block = product[:, (source - first) * width : (source - first + 1) * width]
            partial[source] = block if source else block + bias_ref[...]
    for step in range(parts):
        group = lax.bitwise_xor(place_ref[0], step)
        for tile in range(tiles):
            first = pl.multiple_of((group * tiles + tile) * rows, rows)
            for slot in range(slots):
                source = relative_ref[group * tiles + tile, slot]
                out_refs[step][tile, slot] = partial[source, pl.ds(first, rows), :].astype(out_refs[step].dtype)


def encode(place, relative, bias, x, weights, tiles):
    parts = len(weights)
    tokens, depth = x.shape
    width = bias.shape[1]
    shape = (tiles // parts, relative.shape[1], tokens // tiles, width)
    return pl.pallas_call(
        functools.partial(encode_kernel, parts),
        out_shape=[jax.ShapeDtypeStruct(shape, jnp.bfloat16 if step else jnp.float32) for step in range(parts)],
        in_specs=[SMEM, SMEM] + [VMEM] * (2 + parts),
        out_specs=[VMEM] * parts,
        scratch_shapes=[pltpu.VMEM((parts, tokens, width), jnp.float32)],
        compiler_params=pltpu.CompilerParams(vmem_limit_bytes=24 << 20),
        cost_estimate=pl.CostEstimate(
            flops=2 * tokens * depth * parts * width,
            bytes_accessed=2 * (tokens * depth + depth * parts * width),
            transcendentals=0,
        ),
        name="encode",
    )(place, relative, bias, x, *weights)


def expand(dense, lists_ref, offset, groups_ref, first, act_ref):
    tiles_held, slots, rows, width = act_ref.shape
    tiles = lists_ref.shape[1] // groups_ref.shape[0]
    for held in range(tiles_held):
        for slot in range(slots):
            block = lists_ref[offset, groups_ref[first + held // tiles] * tiles + held % tiles, slot]
            lanes = pl.ds(pl.multiple_of(block * width, width), width)
            dense[held * rows : (held + 1) * rows, lanes] = act_ref[held, slot]


def column_tiles(features):
    columns = 256 if features % 256 == 0 else features
    return [slice(first, first + columns) for first in range(0, features, columns)]


def send_out(stage, out_ref, sems, groups_ref, first, rows, number, lanes):
    copies = []
    for held in range(stage.shape[0] // rows):
        row = pl.multiple_of(groups_ref[first + held] * rows, rows)
        copies.append(
            pltpu.make_async_copy(
                stage.at[held * rows : (held + 1) * rows, lanes],
                out_ref.at[pl.ds(row, rows), lanes],
                sems.at[number, held],
            )
        )
        copies[-1].start()
    return copies


def early_kernel(groups_ref, lists_ref, own_early, own_late, near, far, own_dec, near_dec, far_dec, *refs):
    out_ref, partial_ref, own, others, stage, sems = refs
    half, latents = others[0].shape
    rows = half * 2 // groups_ref.shape[0]
    own[...] = jnp.zeros_like(own)
    others[...] = jnp.zeros_like(others)
    held = groups_ref.shape[0] // 2
    expand(own.at[:half], lists_ref, 0, groups_ref, 0, own_early)
    expand(own.at[half:], lists_ref, 0, groups_ref, held, own_late)
    expand(others.at[0], lists_ref, 1, groups_ref, 0, near)
    expand(others.at[1], lists_ref, 2, groups_ref, 0, far)
    copies = []
    for number, lanes in enumerate(column_tiles(partial_ref.shape[1])):
        total = jnp.dot(own[...], own_dec[:latents, lanes], preferred_element_type=jnp.float32)
        partial_ref[:, lanes] = total[half:]
        total = total[:half] + jnp.dot(others[0], near_dec[:latents, lanes], preferred_element_type=jnp.float32)
        total = total + jnp.dot(others[1], far_dec[:latents, lanes], preferred_element_type=jnp.float32)
        stage[:, lanes] = total.astype(stage.dtype)
        copies += send_out(stage, out_ref, sems, groups_ref, 0, rows, number, lanes)
    for copy in copies:
        copy.wait()


def late_kernel(groups_ref, lists_ref, partial_ref, near, far, near_dec, far_dec, _, out_ref, others, stage, sems):
    half, latents = others[0].shape
    rows = half * 2 // groups_ref.shape[0]
    held = groups_ref.shape[0] // 2
    others[...] = jnp.zeros_like(others)
    expand(others.at[0], lists_ref, 1, groups_ref, held, near)
    expand(others.at[1], lists_ref, 2, groups_ref, held, far)
    copies = []
    for number, lanes in enumerate(column_tiles(partial_ref.shape[1])):
        total = partial_ref[:, lanes] + jnp.dot(others[0], near_dec[:latents, lanes], preferred_element_type=jnp.float32)
        total = total + jnp.dot(others[1], far_dec[:latents, lanes], preferred_element_type=jnp.float32)
        stage[:, lanes] = total.astype(stage.dtype)
        copies += send_out(stage, out_ref, sems, groups_ref, held, rows, number, lanes)
    for copy in copies:
        copy.wait()


def decode_scratch(half, latents, features, parts):
    return [
        pltpu.VMEM((2, half, latents), jnp.bfloat16),
        pltpu.VMEM((half, features), jnp.bfloat16),
        pltpu.SemaphoreType.DMA((len(column_tiles(features)), parts // 2)),
    ]


def decode_early(groups, lists, acts, decoders, tokens):
    latents, features = decoders[0].shape
    half = tokens // 2
    return pl.pallas_call(
        early_kernel,
        out_shape=[
            jax.ShapeDtypeStruct((tokens, features), jnp.bfloat16),
            jax.ShapeDtypeStruct((half, features), jnp.float32),
        ],
        in_specs=[SMEM, SMEM] + [VMEM] * (len(acts) + len(decoders)),
        out_specs=[ANY, VMEM],
        scratch_shapes=[pltpu.VMEM((tokens, latents), jnp.bfloat16)]
        + decode_scratch(half, latents, features, groups.shape[0]),
        compiler_params=pltpu.CompilerParams(vmem_limit_bytes=24 << 20),
        cost_estimate=pl.CostEstimate(
            flops=4 * tokens * latents * features,
            bytes_accessed=2 * (3 * latents * features + 2 * tokens * features),
            transcendentals=0,
        ),
        name="decode_early",
    )(groups, lists, *acts, *decoders)


def decode_late(groups, lists, partial, acts, decoders, rebuilt, latents):
    tokens, features = rebuilt.shape
    return pl.pallas_call(
        late_kernel,
        out_shape=jax.ShapeDtypeStruct((tokens, features), jnp.bfloat16),
        in_specs=[SMEM, SMEM] + [VMEM] * (1 + len(acts) + len(decoders)) + [ANY],
        out_specs=ANY,
        scratch_shapes=decode_scratch(tokens // 2, latents, features, groups.shape[0]),
        input_output_aliases={3 + len(acts) + len(decoders): 0},
        compiler_params=pltpu.CompilerParams(vmem_limit_bytes=24 << 20),
        cost_estimate=pl.CostEstimate(
            flops=2 * tokens * latents * features,
            bytes_accessed=2 * (2 * latents * features + 2 * tokens * features),
            transcendentals=0,
        ),
        name="decode_late",
    )(groups, lists, partial, *acts, *decoders, rebuilt)


def shards(layer_input, enc_weight, enc_bias, dec_weight, block_lists, block_counts):
    parts = lax.axis_size("latent")
    place = lax.axis_index("latent").astype(jnp.int32)
    x, encoder, decoder = layer_input[0], enc_weight[0], dec_weight[0]
    lists, counts = block_lists[0], block_counts[0]
    tokens, depth = x.shape
    tiles, slots = lists.shape
    targets, latents, _ = decoder.shape
    steps, held = doubling(parts)

    if targets != 3:
        raise ValueError("targets")

    with jax.named_scope("encoder_rows"):
        pieces = fetch_rows(place[None], encoder, parts)
        pieces, decoder = lax.optimization_barrier((pieces, decoder))
        weights = [pieces[0]] + [None] * (parts - 1)
        for step in sorted(range(1, parts), reverse=True):
            weights[step] = swapped(pieces[step], step)
    with jax.named_scope("decoder_weights"):
        decoders, all_lists = [decoder[0]], [lists]
        for offset in range(1, targets):
            decoders.append(passed_along(with_lists(decoder[offset], lists), offset))
            all_lists.append(decoders[offset][latents : latents + tiles, :slots].astype(jnp.int32))
        all_lists = jnp.stack(all_lists)

    with jax.named_scope("encode"):
        partials = encode(place[None], lax.bitwise_xor(place, lists), enc_bias, fetch(x), weights, tiles)
        arrived = [swapped(partials[step], step) for step in sorted(range(1, parts), reverse=True)]
    with jax.named_scope("activate"):
        preact = partials[0]
        for term in arrived:
            preact = preact + term.astype(jnp.float32)
        own_counts = lax.dynamic_slice_in_dim(counts, place * (tiles // parts), tiles // parts)
        live = (jnp.arange(slots)[None, :] < own_counts[:, None]).astype(jnp.float32)
        act = (jnp.maximum(preact, 0.0) * live[:, :, None, None]).astype(jnp.bfloat16)
    with jax.named_scope("spread"):
        own = act
        for step in steps[:-1]:
            own = jnp.concatenate([own, swapped(own, step)], axis=0)
        late_own = swapped(own, steps[-1])
        late_own, decoders = lax.optimization_barrier((late_own, decoders))
        even = lax.axis_index("layer") % 2 == 0
        far = passed_along(own, 2)
        late_far = passed_along(late_own, 2)
        near = across_cores(jnp.where(even, own, far))
    with jax.named_scope("decode"):
        groups = lax.bitwise_xor(place, jnp.array(held, jnp.int32))
        rebuilt, partial = decode_early(groups, all_lists, [own, late_own, near, far], decoders, tokens)
        rebuilt, partial, late_far = lax.optimization_barrier((rebuilt, partial, late_far))
        late = [across_cores(jnp.where(even, late_own, late_far)), late_far]
        return decode_late(groups, all_lists, partial, late, decoders[1:], rebuilt, latents)[None]


def solution(mesh):
    placed = (
        P("layer", None, "latent"),
        P("layer", None, "latent"),
        P("layer", "latent"),
        P("layer", None, None, "latent"),
        P("layer", None, None),
        P("layer", None),
    )
    return jax.shard_map(
        shards, mesh=mesh, in_specs=placed, out_specs=P("layer", None, "latent"), check_vma=False
    )
```

profile of v0, /device:TPU:5, one launch (start us, length us, event | category | flops | bytes accessed | tf_op | source)
XLA Modules:
  0.0 112.8 jit_solution(14078213504028931387)
XLA Ops:
  0.0 32.9 %fetch_rows.1 = (bf16[1024,128]{1,0:T(8,128)(2,1)}, bf16[1024,128]{1,0:T(8,128)(2,1)}, bf16[1024,128]{1,0:T(8,128)(2,1)}, bf16[1024,128]{1,0:T(8,128)(2,1)}) custom-call(s32[1]{0:T(128)} %bitcast.place_ref, bf16[4096,128]{1,0:T(8,128)(2,1)} %bitcast.21), custom_call_target="tpu_custom_call" | custom-call | tf_op jit(solution)/shard_map/encoder_rows/fetch_rows/pallas_call | solution.py:54
  32.9 1.4 %collective-permute-start.2 = (bf16[1024,128]{1,0:T(8,128)(2,1)}, bf16[1024,128]{1,0:T(8,128)(2,1)}, u32[]{:S(2)}, u32[]{:S(2)}) collective-permute-start(bf16[1024,128]{1,0:T(8,128)(2,1)} %get-tuple-element.33), channel_id=1, source_target_pairs={{0,1},{1,0},{2,3},{3,2},{4,5},{5,4},{6,7},{7,6},{8,9},{9,8},{10,11... | collective-permute-start | bytes 786440 | tf_op jit(solution)/shard_map/encoder_rows/ppermute | solution.py:17
  34.3 2.3 %collective-permute-start.3 = (bf16[1024,128]{1,0:T(8,128)(2,1)}, bf16[1024,128]{1,0:T(8,128)(2,1)}, u32[]{:S(2)}, u32[]{:S(2)}) collective-permute-start(bf16[1024,128]{1,0:T(8,128)(2,1)} %get-tuple-element.34), channel_id=1, source_target_pairs={{0,2},{1,3},{2,0},{3,1},{4,6},{5,7},{6,4},{7,5},{8,10},{9,11},{10,... | collective-permute-start | bytes 786440 | tf_op jit(solution)/shard_map/encoder_rows/ppermute | solution.py:17
  36.6 0.0 collective-permute-start.4
  36.6 0.8 xor_bitcast_fusion
  37.3 0.1 copy.22
  37.4 3.1 %slice_bitcast_fusion = (bf16[512,1024]{1,0:T(8,128)(2,1)}, bf16[512,1024]{1,0:T(8,128)(2,1)S(1)}, bf16[512,1024]{1,0:T(8,128)(2,1)S(1)}) fusion(bf16[3,512,1024]{2,1,0:T(8,128)(2,1)} %bitcast.20), kind=kLoop, calls=%fused_computation.4 | loop fusion | bytes 6291456 | tf_op jit(solution)/shard_map/decoder_weights/squeeze | solution.py:271
  40.6 1.5 %fusion.1 = (bf16[528,1024]{1,0:T(8,128)(2,1)}, bf16[528,1024]{1,0:T(8,128)(2,1)}) fusion(bf16[16,2]{1,0:T(8,128)(2,1)S(1)} %copy.22, bf16[512,1024]{1,0:T(8,128)(2,1)S(1)} %get-tuple-element.51, bf16[512,1024]{1,0:T(8,128)(2,1)S(1)} %get-tuple-element.50), kind=kLoop, calls=%fused_computation.2 | loop fusion | flops 4866048 | bytes 4259904 | tf_op jit(solution)/shard_map/decoder_weights/concatenate | solution.py:86
  42.1 4.5 %collective-permute-start = (bf16[528,1024]{1,0:T(8,128)(2,1)}, bf16[528,1024]{1,0:T(8,128)(2,1)S(1)}, u32[]{:S(2)}, u32[]{:S(2)}) collective-permute-start(bf16[528,1024]{1,0:T(8,128)(2,1)} %get-tuple-element.52), channel_id=1, source_target_pairs={{0,4},{4,8},{8,12},{12,16},{16,20},{20,24},{24,28},{1,5},{5,9},{9,... | collective-permute-start | bytes 3244040 | tf_op jit(solution)/shard_map/decoder_weights/ppermute | solution.py:22
  46.6 1.9 %collective-permute-start.1 = (bf16[528,1024]{1,0:T(8,128)(2,1)}, bf16[528,1024]{1,0:T(8,128)(2,1)}, u32[]{:S(2)}, u32[]{:S(2)}) collective-permute-start(bf16[528,1024]{1,0:T(8,128)(2,1)} %get-tuple-element.53), channel_id=1, source_target_pairs={{0,8},{4,12},{8,16},{12,20},{16,24},{20,28},{1,9},{5,13},{9,17},{1... | collective-permute-start | bytes 3244040 | tf_op jit(solution)/shard_map/decoder_weights/ppermute | solution.py:22
  48.5 0.1 copy.25.relative_ref
  48.6 0.2 fetch.1.x_ref
  48.7 0.0 copy-start.2
  48.8 1.3 %copy-done.2 = bf16[1024,1024]{1,0:T(8,128)(2,1)} copy-done((bf16[1024,1024]{1,0:T(8,128)(2,1)}, bf16[1024,1024]{1,0:T(8,128)(2,1)S(1)}, u32[]{:S(2)}) %copy-start.2) | copy-done | bytes 2097176
  50.1 0.1 dynamic-slice_bitcast_fusion
  50.1 0.0 collective-permute-done.2.refs_1_
  50.2 0.0 collective-permute-done.3.refs_2_
  50.2 3.6 %collective-permute-done.4.refs_3_ = bf16[1024,128]{1,0:T(8,128)(2,1)} collective-permute-done((bf16[1024,128]{1,0:T(8,128)(2,1)}, bf16[1024,128]{1,0:T(8,128)(2,1)}, u32[]{:S(2)}, u32[]{:S(2)}) %collective-permute-start.4) | collective-permute-done | bytes 262176 | tf_op jit(solution)/shard_map/encoder_rows/ppermute | solution.py:17
  53.8 1.6 %copy-done.3 = bf16[1024,1024]{1,0:T(8,128)(2,1)S(1)} copy-done((bf16[1024,1024]{1,0:T(8,128)(2,1)S(1)}, bf16[1024,1024]{1,0:T(8,128)(2,1)}, u32[]{:S(2)}) %copy-start.3) | copy-done | bytes 2097176
  55.4 2.4 %encode.1 = (f32[4,2,64,128]{3,2,1,0:T(8,128)S(1)}, bf16[4,2,64,128]{3,2,1,0:T(8,128)(2,1)S(1)}, bf16[4,2,64,128]{3,2,1,0:T(8,128)(2,1)S(1)}, bf16[4,2,64,128]{3,2,1,0:T(8,128)(2,1)S(1)}) custom-call(s32[1]{0:T(128)} %bitcast.place_ref, s32[16,2]{1,0:T(8,128)S(1)} %copy.25.relative_ref, f32[1,128]{1,0:T(1,128)S(1)} %copy-done.6, ...), custom_call_target="tpu_custom_call" | custom-call | flops 1073741824 | bytes 3145728 | tf_op jit(solution)/shard_map/encode/encode/pallas_call | solution.py:115
  57.8 1.1 %collective-permute-start.5 = (bf16[4,2,64,128]{3,2,1,0:T(8,128)(2,1)S(1)}, bf16[4,2,64,128]{3,2,1,0:T(8,128)(2,1)S(1)}, u32[]{:S(2)}, u32[]{:S(2)}) collective-permute-start(bf16[4,2,64,128]{3,2,1,0:T(8,128)(2,1)S(1)} %get-tuple-element.37), channel_id=1, source_target_pairs={{0,3},{1,2},{2,1},{3,0},{4,7},{5,6},{6,5},{7,4},{8,11},{9,10},{10,... | collective-permute-start | bytes 393224 | tf_op jit(solution)/shard_map/encode/ppermute | solution.py:17
  58.9 5.9 %collective-permute-start.6 = (bf16[4,2,64,128]{3,2,1,0:T(8,128)(2,1)S(1)}, bf16[4,2,64,128]{3,2,1,0:T(8,128)(2,1)S(1)}, u32[]{:S(2)}, u32[]{:S(2)}) collective-permute-start(bf16[4,2,64,128]{3,2,1,0:T(8,128)(2,1)S(1)} %get-tuple-element.38), channel_id=1, source_target_pairs={{0,2},{1,3},{2,0},{3,1},{4,6},{5,7},{6,4},{7,5},{8,10},{9,11},{10,... | collective-permute-start | bytes 393224 | tf_op jit(solution)/shard_map/encode/ppermute | solution.py:17
  64.9 0.1 collective-permute-start.7
  65.0 0.1 fusion.3
  65.0 0.0 collective-permute-done.5
  65.0 9.8 %collective-permute-done.6 = bf16[4,2,64,128]{3,2,1,0:T(8,128)(2,1)S(1)} collective-permute-done((bf16[4,2,64,128]{3,2,1,0:T(8,128)(2,1)S(1)}, bf16[4,2,64,128]{3,2,1,0:T(8,128)(2,1)S(1)}, u32[]{:S(2)}, u32[]{:S(2)}) %collective-permute-start.6) | collective-permute-done | bytes 131104 | tf_op jit(solution)/shard_map/encode/ppermute | solution.py:17
  74.9 0.0 collective-permute-done.7
  74.9 0.1 multiply_convert_fusion
  75.0 0.1 collective-permute-start.8
  75.1 8.3 %collective-permute-done.8 = bf16[4,2,64,128]{3,2,1,0:T(8,128)(2,1)S(1)} collective-permute-done((bf16[4,2,64,128]{3,2,1,0:T(8,128)(2,1)S(1)}, bf16[4,2,64,128]{3,2,1,0:T(8,128)(2,1)S(1)}, u32[]{:S(2)}, u32[]{:S(2)}) %collective-permute-start.8) | collective-permute-done | bytes 131104 | tf_op jit(solution)/shard_map/spread/ppermute | solution.py:17
  83.4 3.0 %collective-permute-start.10 = (bf16[8,2,64,128]{3,2,1,0:T(8,128)(2,1)S(1)}, bf16[8,2,64,128]{3,2,1,0:T(8,128)(2,1)S(1)}, u32[]{:S(2)}, u32[]{:S(2)}) collective-permute-start(bf16[8,2,64,128]{3,2,1,0:T(8,128)(2,1)S(1)} %pad_maximum_fusion.own_early), channel_id=1, source_target_pairs={{0,8},{4,12},{8,16},{12,20},{16,24},{20,28},{1,9},{5,13},{9,17},{1... | collective-permute-start | bytes 786440 | tf_op jit(solution)/shard_map/spread/ppermute | solution.py:22
  86.4 0.1 collective-permute-start.9
  86.5 6.1 %collective-permute-done.10.far = bf16[8,2,64,128]{3,2,1,0:T(8,128)(2,1)S(1)} collective-permute-done((bf16[8,2,64,128]{3,2,1,0:T(8,128)(2,1)S(1)}, bf16[8,2,64,128]{3,2,1,0:T(8,128)(2,1)S(1)}, u32[]{:S(2)}, u32[]{:S(2)}) %collective-permute-start.10) | collective-permute-done | bytes 262176 | tf_op jit(solution)/shard_map/spread/ppermute | solution.py:22
  92.6 0.7 broadcast_select_fusion.1
  93.4 2.3 %collective-permute-start.11 = (bf16[8,2,64,128]{3,2,1,0:T(8,128)(2,1)}, bf16[8,2,64,128]{3,2,1,0:T(8,128)(2,1)S(1)}, u32[]{:S(2)}, u32[]{:S(2)}) collective-permute-start(bf16[8,2,64,128]{3,2,1,0:T(8,128)(2,1)} %broadcast_select_fusion.1), channel_id=1, source_target_pairs={{0,4},{4,0},{8,12},{12,8},{16,20},{20,16},{24,28},{28,24},{1,5},{5... | collective-permute-start | bytes 786440 | tf_op jit(solution)/shard_map/spread/ppermute | solution.py:27
  95.6 0.0 collective-permute-done.near_dec
  95.6 0.1 copy.23
  95.7 0.0 collective-permute-done.9.own_late
  95.7 0.7 slice_convert_fusion
  96.4 0.1 copy.24
  96.5 2.1 %collective-permute-start.12 = (bf16[8,2,64,128]{3,2,1,0:T(8,128)(2,1)S(1)}, bf16[8,2,64,128]{3,2,1,0:T(8,128)(2,1)S(1)}, u32[]{:S(2)}, u32[]{:S(2)}) collective-permute-start(bf16[8,2,64,128]{3,2,1,0:T(8,128)(2,1)S(1)} %collective-permute-done.9.own_late), channel_id=1, source_target_pairs={{0,8},{4,12},{8,16},{12,20},{16,24},{20,28},{1,9},{5,13},{9,17},{1... | collective-permute-start | bytes 786440 | tf_op jit(solution)/shard_map/spread/ppermute | solution.py:22
  98.6 0.1 copy.27.lists_ref
  98.7 0.0 collective-permute-done.11.near
  98.7 4.7 %decode_early.1 = (bf16[1024,1024]{1,0:T(8,128)(2,1)}, f32[512,1024]{1,0:T(8,128)S(1)}) custom-call(s32[4]{0:T(128)S(1)} %broadcast_xor_fusion.groups_ref, s32[3,16,2]{2,1,0:T(8,128)S(1)} %copy.27.lists_ref, bf16[8,2,64,128]{3,2,1,0:T(8,128)(2,1)S(1)} %pad_maximum_fusion.own_early, bf16[8,2,64,128]{3,2,1,0:T(8,128)(2,1)S(1)} %collective-permute-done.9.own_late, ...), custom_call_target="tpu_custom_call" | custom-call | flops 2147483648 | bytes 7340032 | tf_op jit(solution)/shard_map/decode/decode_early/pallas_call | solution.py:212
  103.4 3.8 %collective-permute-done.12.far = bf16[8,2,64,128]{3,2,1,0:T(8,128)(2,1)S(1)} collective-permute-done((bf16[8,2,64,128]{3,2,1,0:T(8,128)(2,1)S(1)}, bf16[8,2,64,128]{3,2,1,0:T(8,128)(2,1)S(1)}, u32[]{:S(2)}, u32[]{:S(2)}) %collective-permute-start.12) | collective-permute-done | bytes 262176 | tf_op jit(solution)/shard_map/spread/ppermute | solution.py:22
  107.2 0.8 collective-permute-start.13
  108.1 1.2 %collective-permute-done.13.near = bf16[8,2,64,128]{3,2,1,0:T(8,128)(2,1)S(1)} collective-permute-done((bf16[8,2,64,128]{3,2,1,0:T(8,128)(2,1)S(1)}, bf16[8,2,64,128]{3,2,1,0:T(8,128)(2,1)S(1)}, u32[]{:S(2)}, u32[]{:S(2)}) %collective-permute-start.13) | collective-permute-done | bytes 262176 | tf_op jit(solution)/shard_map/decode/ppermute | solution.py:27
  109.2 3.6 %decode_late.1 = bf16[1024,1024]{1,0:T(8,128)(2,1)} custom-call(s32[4]{0:T(128)S(1)} %broadcast_xor_fusion.groups_ref, s32[3,16,2]{2,1,0:T(8,128)S(1)} %copy.27.lists_ref, f32[512,1024]{1,0:T(8,128)S(1)} %get-tuple-element.46.partial_ref, bf16[8,2,64,128]{3,2,1,0:T(8,128)(2,1)S(1)} %collective-permute-done.13.near, ...), custom_call_target="tpu_custom_call", output_to_operand_aliasing={{}: (7, {})} | custom-call | flops 1073741824 | bytes 6291456 | tf_op jit(solution)/shard_map/decode/decode_late/pallas_call | solution.py:234
  (21 shorter events, 0.1 us)
Async XLA Ops:
  0.0 50.1 %copy-start = (s32[1,16]{1,0:T(1,128)S(1)}, s32[1,16]{1,0:T(1,128)}, u32[]{:S(2)}) copy-start(s32[1,16]{1,0:T(1,128)} %param.12) | copy-start | bytes 196
  32.9 17.2 %collective-permute-start.2 = (bf16[1024,128]{1,0:T(8,128)(2,1)}, bf16[1024,128]{1,0:T(8,128)(2,1)}, u32[]{:S(2)}, u32[]{:S(2)}) collective-permute-start(bf16[1024,128]{1,0:T(8,128)(2,1)} %get-tuple-element.33), channel_id=1, source_target_pairs={{0,1},{1,0},{2,3},{3,2},{4,5},{5,4},{6,7},{7,6},{8,9},{9,8},{10,11... | collective-permute-start | bytes 786440 | tf_op jit(solution)/shard_map/encoder_rows/ppermute | solution.py:17
  34.3 15.9 %collective-permute-start.3 = (bf16[1024,128]{1,0:T(8,128)(2,1)}, bf16[1024,128]{1,0:T(8,128)(2,1)}, u32[]{:S(2)}, u32[]{:S(2)}) collective-permute-start(bf16[1024,128]{1,0:T(8,128)(2,1)} %get-tuple-element.34), channel_id=1, source_target_pairs={{0,2},{1,3},{2,0},{3,1},{4,6},{5,7},{6,4},{7,5},{8,10},{9,11},{10,... | collective-permute-start | bytes 786440 | tf_op jit(solution)/shard_map/encoder_rows/ppermute | solution.py:17
  36.6 17.2 %collective-permute-start.4 = (bf16[1024,128]{1,0:T(8,128)(2,1)}, bf16[1024,128]{1,0:T(8,128)(2,1)}, u32[]{:S(2)}, u32[]{:S(2)}) collective-permute-start(bf16[1024,128]{1,0:T(8,128)(2,1)} %get-tuple-element.35), channel_id=1, source_target_pairs={{0,3},{1,2},{2,1},{3,0},{4,7},{5,6},{6,5},{7,4},{8,11},{9,10},{10,... | collective-permute-start | bytes 786440 | tf_op jit(solution)/shard_map/encoder_rows/ppermute | solution.py:17
  40.6 8.0 %copy-start.1 = (bf16[1,1024,1024]{2,1,0:T(8,128)(2,1)S(1)}, bf16[1,1024,1024]{2,1,0:T(8,128)(2,1)}, u32[]{:S(2)}) copy-start(bf16[1,1024,1024]{2,1,0:T(8,128)(2,1)} %param.7) | copy-start | bytes 6291460
  42.1 53.5 %collective-permute-start = (bf16[528,1024]{1,0:T(8,128)(2,1)}, bf16[528,1024]{1,0:T(8,128)(2,1)S(1)}, u32[]{:S(2)}, u32[]{:S(2)}) collective-permute-start(bf16[528,1024]{1,0:T(8,128)(2,1)} %get-tuple-element.52), channel_id=1, source_target_pairs={{0,4},{4,8},{8,12},{12,16},{16,20},{20,24},{24,28},{1,5},{5,9},{9,... | collective-permute-start | bytes 3244040 | tf_op jit(solution)/shard_map/decoder_weights/ppermute | solution.py:22
  46.6 49.1 %collective-permute-start.1 = (bf16[528,1024]{1,0:T(8,128)(2,1)}, bf16[528,1024]{1,0:T(8,128)(2,1)}, u32[]{:S(2)}, u32[]{:S(2)}) collective-permute-start(bf16[528,1024]{1,0:T(8,128)(2,1)} %get-tuple-element.53), channel_id=1, source_target_pairs={{0,8},{4,12},{8,16},{12,20},{16,24},{20,28},{1,9},{5,13},{9,17},{1... | collective-permute-start | bytes 3244040 | tf_op jit(solution)/shard_map/decoder_weights/ppermute | solution.py:22
  48.6 5.2 %copy-start.5 = (bf16[1024,128]{1,0:T(8,128)(2,1)S(1)}, bf16[1024,128]{1,0:T(8,128)(2,1)}, u32[]{:S(2)}) copy-start(bf16[1024,128]{1,0:T(8,128)(2,1)} %get-tuple-element.32.refs_0_) | copy-start | bytes 786436
  48.6 5.2 %copy-start.6 = (f32[1,128]{1,0:T(1,128)S(1)}, f32[1,128]{1,0:T(1,128)}, u32[]{:S(2)}) copy-start(f32[1,128]{1,0:T(1,128)} %bias_ref.1) | copy-start | bytes 1540
  48.7 1.3 %copy-start.2 = (bf16[1024,1024]{1,0:T(8,128)(2,1)}, bf16[1024,1024]{1,0:T(8,128)(2,1)S(1)}, u32[]{:S(2)}) copy-start(bf16[1024,1024]{1,0:T(8,128)(2,1)S(1)} %fetch.1.x_ref) | copy-start | bytes 6291460
  50.1 36.3 %copy-start.8 = (s32[4]{0:T(128)S(1)}, s32[4]{0:T(128)}, u32[]{:S(2)}) copy-start(s32[4]{0:T(128)} %constant.34.clone) | copy-start | bytes 52
  50.1 48.5 %copy-start.7 = (s32[1,16,2]{1,2,0:T(2,128)S(1)}, s32[1,16,2]{1,2,0:T(2,128)}, u32[]{:S(2)}) copy-start(s32[1,16,2]{1,2,0:T(2,128)} %param.11) | copy-start | bytes 388
  53.8 1.6 %copy-start.3 = (bf16[1024,1024]{1,0:T(8,128)(2,1)S(1)}, bf16[1024,1024]{1,0:T(8,128)(2,1)}, u32[]{:S(2)}) copy-start(bf16[1024,1024]{1,0:T(8,128)(2,1)} %copy-done.2) | copy-start | bytes 6291460
  57.8 40.9 %copy-start.4 = (bf16[512,1024]{1,0:T(8,128)(2,1)S(1)}, bf16[512,1024]{1,0:T(8,128)(2,1)}, u32[]{:S(2)}) copy-start(bf16[512,1024]{1,0:T(8,128)(2,1)} %get-tuple-element.41.own_dec) | copy-start | bytes 3145732
  57.8 7.2 %collective-permute-start.5 = (bf16[4,2,64,128]{3,2,1,0:T(8,128)(2,1)S(1)}, bf16[4,2,64,128]{3,2,1,0:T(8,128)(2,1)S(1)}, u32[]{:S(2)}, u32[]{:S(2)}) collective-permute-start(bf16[4,2,64,128]{3,2,1,0:T(8,128)(2,1)S(1)} %get-tuple-element.37), channel_id=1, source_target_pairs={{0,3},{1,2},{2,1},{3,0},{4,7},{5,6},{6,5},{7,4},{8,11},{9,10},{10,... | collective-permute-start | bytes 393224 | tf_op jit(solution)/shard_map/encode/ppermute | solution.py:17
  58.9 15.9 %collective-permute-start.6 = (bf16[4,2,64,128]{3,2,1,0:T(8,128)(2,1)S(1)}, bf16[4,2,64,128]{3,2,1,0:T(8,128)(2,1)S(1)}, u32[]{:S(2)}, u32[]{:S(2)}) collective-permute-start(bf16[4,2,64,128]{3,2,1,0:T(8,128)(2,1)S(1)} %get-tuple-element.38), channel_id=1, source_target_pairs={{0,2},{1,3},{2,0},{3,1},{4,6},{5,7},{6,4},{7,5},{8,10},{9,11},{10,... | collective-permute-start | bytes 393224 | tf_op jit(solution)/shard_map/encode/ppermute | solution.py:17
  64.9 10.0 %collective-permute-start.7 = (bf16[4,2,64,128]{3,2,1,0:T(8,128)(2,1)S(1)}, bf16[4,2,64,128]{3,2,1,0:T(8,128)(2,1)S(1)}, u32[]{:S(2)}, u32[]{:S(2)}) collective-permute-start(bf16[4,2,64,128]{3,2,1,0:T(8,128)(2,1)S(1)} %get-tuple-element.39), channel_id=1, source_target_pairs={{0,1},{1,0},{2,3},{3,2},{4,5},{5,4},{6,7},{7,6},{8,9},{9,8},{10,11... | collective-permute-start | bytes 393224 | tf_op jit(solution)/shard_map/encode/ppermute | solution.py:17
  75.0 8.3 %collective-permute-start.8 = (bf16[4,2,64,128]{3,2,1,0:T(8,128)(2,1)S(1)}, bf16[4,2,64,128]{3,2,1,0:T(8,128)(2,1)S(1)}, u32[]{:S(2)}, u32[]{:S(2)}) collective-permute-start(bf16[4,2,64,128]{3,2,1,0:T(8,128)(2,1)S(1)} %multiply_convert_fusion), channel_id=1, source_target_pairs={{0,2},{1,3},{2,0},{3,1},{4,6},{5,7},{6,4},{7,5},{8,10},{9,11},{10,... | collective-permute-start | bytes 393224 | tf_op jit(solution)/shard_map/spread/ppermute | solution.py:17
  83.4 9.3 %collective-permute-start.10 = (bf16[8,2,64,128]{3,2,1,0:T(8,128)(2,1)S(1)}, bf16[8,2,64,128]{3,2,1,0:T(8,128)(2,1)S(1)}, u32[]{:S(2)}, u32[]{:S(2)}) collective-permute-start(bf16[8,2,64,128]{3,2,1,0:T(8,128)(2,1)S(1)} %pad_maximum_fusion.own_early), channel_id=1, source_target_pairs={{0,8},{4,12},{8,16},{12,20},{16,24},{20,28},{1,9},{5,13},{9,17},{1... | collective-permute-start | bytes 786440 | tf_op jit(solution)/shard_map/spread/ppermute | solution.py:22
  86.4 9.3 %collective-permute-start.9 = (bf16[8,2,64,128]{3,2,1,0:T(8,128)(2,1)S(1)}, bf16[8,2,64,128]{3,2,1,0:T(8,128)(2,1)S(1)}, u32[]{:S(2)}, u32[]{:S(2)}) collective-permute-start(bf16[8,2,64,128]{3,2,1,0:T(8,128)(2,1)S(1)} %pad_maximum_fusion.own_early), channel_id=1, source_target_pairs={{0,1},{1,0},{2,3},{3,2},{4,5},{5,4},{6,7},{7,6},{8,9},{9,8},{10,11... | collective-permute-start | bytes 786440 | tf_op jit(solution)/shard_map/spread/ppermute | solution.py:17
  93.4 5.4 %collective-permute-start.11 = (bf16[8,2,64,128]{3,2,1,0:T(8,128)(2,1)}, bf16[8,2,64,128]{3,2,1,0:T(8,128)(2,1)S(1)}, u32[]{:S(2)}, u32[]{:S(2)}) collective-permute-start(bf16[8,2,64,128]{3,2,1,0:T(8,128)(2,1)} %broadcast_select_fusion.1), channel_id=1, source_target_pairs={{0,4},{4,0},{8,12},{12,8},{16,20},{20,16},{24,28},{28,24},{1,5},{5... | collective-permute-start | bytes 786440 | tf_op jit(solution)/shard_map/spread/ppermute | solution.py:27
  96.5 10.7 %collective-permute-start.12 = (bf16[8,2,64,128]{3,2,1,0:T(8,128)(2,1)S(1)}, bf16[8,2,64,128]{3,2,1,0:T(8,128)(2,1)S(1)}, u32[]{:S(2)}, u32[]{:S(2)}) collective-permute-start(bf16[8,2,64,128]{3,2,1,0:T(8,128)(2,1)S(1)} %collective-permute-done.9.own_late), channel_id=1, source_target_pairs={{0,8},{4,12},{8,16},{12,20},{16,24},{20,28},{1,9},{5,13},{9,17},{1... | collective-permute-start | bytes 786440 | tf_op jit(solution)/shard_map/spread/ppermute | solution.py:22
  107.2 2.0 %collective-permute-start.13 = (bf16[8,2,64,128]{3,2,1,0:T(8,128)(2,1)S(1)}, bf16[8,2,64,128]{3,2,1,0:T(8,128)(2,1)S(1)}, u32[]{:S(2)}, u32[]{:S(2)}) collective-permute-start(bf16[8,2,64,128]{3,2,1,0:T(8,128)(2,1)S(1)} %broadcast_select_fusion), channel_id=1, source_target_pairs={{0,4},{4,0},{8,12},{12,8},{16,20},{20,16},{24,28},{28,24},{1,5},{5... | collective-permute-start | bytes 786440 | tf_op jit(solution)/shard_map/decode/ppermute | solution.py:27
where the time goes:
time: 113 us
  Pallas kernels  43.7 us (39%)
  waiting for transfers between devices  32.8 us (29%)
  starting transfers between devices  25.6 us (23%)
  local copies, waits for them, and re-layouts  6.59 us (6%)
  other arithmetic  3.93 us (3%)
    pallas_call x1, Pallas kernels, fetch_rows(): pl.pallas_call(fetch_rows_kernel, out_shape=[jax.ShapeDtypeStruct((depth,...  32.9 us
    ppermute x8, waiting for transfers between devices, swapped(): return lax.ppermute(value, 'latent', [(i, i ^ step) for i in range(count)])  21.7 us
    ppermute x4, starting transfers between devices, passed_along(): lax.ppermute(value, 'layer', [(i, i + steps) for i in range(count - steps)])  11.5 us
    ppermute x8, starting transfers between devices, swapped(): return lax.ppermute(value, 'latent', [(i, i ^ step) for i in range(count)])  11 us
    ppermute x4, waiting for transfers between devices, passed_along(): lax.ppermute(value, 'layer', [(i, i + steps) for i in range(count - steps)])  9.89 us
    pallas_call x1, Pallas kernels, decode_early(): pl.pallas_call(early_kernel, out_shape=[jax.ShapeDtypeStruct((tokens, fea...  4.71 us
    pallas_call x1, Pallas kernels, decode_late(): pl.pallas_call(late_kernel, out_shape=jax.ShapeDtypeStruct((tokens, featu...  3.57 us
    squeeze x1, local copies, waits for them, and re-layouts, shards(): decoders, all_lists = ([decoder[0]], [lists])  3.14 us
  transfers between devices with their start and end apart: 14, of which 6 were waited for; matrix products, arithmetic and copies ran while one was open for 7% of the time, Pallas kernels for 6%

commit v1 on v0

--- a/solution.py
+++ b/solution.py
@@ -10,6 +10,7 @@
 VMEM = pl.BlockSpec(memory_space=pltpu.VMEM)
 SMEM = pl.BlockSpec(memory_space=pltpu.SMEM)
 ANY = pl.BlockSpec(memory_space=pl.ANY)
+HBM = pl.BlockSpec(memory_space=pltpu.HBM)
 
 
 def swapped(value, step):
@@ -54,30 +55,12 @@
     return pl.pallas_call(
         fetch_rows_kernel,
         out_shape=[jax.ShapeDtypeStruct((depth, encoder.shape[1]), encoder.dtype)] * parts,
-        in_specs=[SMEM, ANY],
-        out_specs=[ANY] * parts,
+        in_specs=[SMEM, HBM],
+        out_specs=[VMEM] * parts,
         scratch_shapes=[pltpu.SemaphoreType.DMA((parts,))],
-        compiler_params=pltpu.CompilerParams(vmem_limit_bytes=60 << 20),
+        compiler_params=pltpu.CompilerParams(vmem_limit_bytes=16 << 20),
         name="fetch_rows",
     )(place, encoder)
-
-
-def fetch_kernel(source_ref, out_ref, sem):
-    copy = pltpu.make_async_copy(source_ref, out_ref, sem)
-    copy.start()
-    copy.wait()
-
-
-def fetch(value):
-    return pl.pallas_call(
-        fetch_kernel,
-        out_shape=jax.ShapeDtypeStruct(value.shape, value.dtype),
-        in_specs=[ANY],
-        out_specs=VMEM,
-        scratch_shapes=[pltpu.SemaphoreType.DMA],
-        compiler_params=pltpu.CompilerParams(vmem_limit_bytes=48 << 20),
-        name="fetch",
-    )(value)
 
 
 def with_lists(decoder, lists):
@@ -86,25 +69,33 @@
     return jnp.concatenate([decoder, ids], axis=0)
 
 
-def encode_kernel(parts, place_ref, relative_ref, bias_ref, x_ref, *refs):
+def encode_kernel(parts, place_ref, relative_ref, bias_ref, x_hbm, *refs):
     weight_refs, refs = refs[:parts], refs[parts:]
-    out_refs, partial = refs[:parts], refs[parts]
+    out_refs, (x_ref, partial, sems) = refs[:parts], refs[parts:]
     width = bias_ref.shape[1]
     tiles, slots, rows, _ = out_refs[0].shape
+    group_rows = tiles * rows
+    copies = []
+    for step in range(parts):
+        group = pl.ds(pl.multiple_of(lax.bitwise_xor(place_ref[0], step) * group_rows, group_rows), group_rows)
+        copies.append(pltpu.make_async_copy(x_hbm.at[group], x_ref.at[step], sems.at[step]))
+    for copy in reversed(copies):
+        copy.start()
     pair = 1 + (parts > 1)
-    for first in range(0, parts, pair):
-        stacked = jnp.concatenate([ref[...] for ref in weight_refs[first : first + pair]], axis=1)
-        product = jnp.dot(x_ref[...], stacked, preferred_element_type=jnp.float32)
-        for source in range(first, first + pair):
-            block = product[:, (source - first) * width : (source - first + 1) * width]
-            partial[source] = block if source else block + bias_ref[...]
-    for step in range(parts):
+    for step in reversed(range(parts)):
+        copies[step].wait()
+        for first in range(0, parts, pair):
+            stacked = jnp.concatenate([ref[...] for ref in weight_refs[first : first + pair]], axis=1)
+            product = jnp.dot(x_ref[step], stacked, preferred_element_type=jnp.float32)
+            for source in range(first, first + pair):
+                block = product[:, (source - first) * width : (source - first + 1) * width]
+                partial[source] = block if source else block + bias_ref[...]
         group = lax.bitwise_xor(place_ref[0], step)
         for tile in range(tiles):
-            first = pl.multiple_of((group * tiles + tile) * rows, rows)
             for slot in range(slots):
                 source = relative_ref[group * tiles + tile, slot]
-                out_refs[step][tile, slot] = partial[source, pl.ds(first, rows), :].astype(out_refs[step].dtype)
+                kept = partial[source, tile * rows : (tile + 1) * rows, :]
+                out_refs[step][tile, slot] = kept.astype(out_refs[step].dtype)
 
 
 def encode(place, relative, bias, x, weights, tiles):
@@ -115,10 +106,14 @@
     return pl.pallas_call(
         functools.partial(encode_kernel, parts),
         out_shape=[jax.ShapeDtypeStruct(shape, jnp.bfloat16 if step else jnp.float32) for step in range(parts)],
-        in_specs=[SMEM, SMEM] + [VMEM] * (2 + parts),
+        in_specs=[SMEM, SMEM, VMEM, HBM] + [VMEM] * parts,
         out_specs=[VMEM] * parts,
-        scratch_shapes=[pltpu.VMEM((parts, tokens, width), jnp.float32)],
-        compiler_params=pltpu.CompilerParams(vmem_limit_bytes=24 << 20),
+        scratch_shapes=[
+            pltpu.VMEM((parts, tokens // parts, depth), x.dtype),
+            pltpu.VMEM((parts, tokens // parts, width), jnp.float32),
+            pltpu.SemaphoreType.DMA((parts,)),
+        ],
+        compiler_params=pltpu.CompilerParams(vmem_limit_bytes=16 << 20),
         cost_estimate=pl.CostEstimate(
             flops=2 * tokens * depth * parts * width,
             bytes_accessed=2 * (tokens * depth + depth * parts * width),
@@ -219,7 +214,7 @@
         out_specs=[ANY, VMEM],
         scratch_shapes=[pltpu.VMEM((tokens, latents), jnp.bfloat16)]
         + decode_scratch(half, latents, features, groups.shape[0]),
-        compiler_params=pltpu.CompilerParams(vmem_limit_bytes=24 << 20),
+        compiler_params=pltpu.CompilerParams(vmem_limit_bytes=16 << 20),
         cost_estimate=pl.CostEstimate(
             flops=4 * tokens * latents * features,
             bytes_accessed=2 * (3 * latents * features + 2 * tokens * features),
@@ -238,7 +233,7 @@
         out_specs=ANY,
         scratch_shapes=decode_scratch(tokens // 2, latents, features, groups.shape[0]),
         input_output_aliases={3 + len(acts) + len(decoders): 0},
-        compiler_params=pltpu.CompilerParams(vmem_limit_bytes=24 << 20),
+        compiler_params=pltpu.CompilerParams(vmem_limit_bytes=16 << 20),
         cost_estimate=pl.CostEstimate(
             flops=2 * tokens * latents * features,
             bytes_accessed=2 * (2 * latents * features + 2 * tokens * features),
@@ -275,7 +270,7 @@
         all_lists = jnp.stack(all_lists)
 
     with jax.named_scope("encode"):
-        partials = encode(place[None], lax.bitwise_xor(place, lists), enc_bias, fetch(x), weights, tiles)
+        partials = encode(place[None], lax.bitwise_xor(place, lists), enc_bias, x, weights, tiles)
         arrived = [swapped(partials[step], step) for step in sorted(range(1, parts), reverse=True)]
     with jax.named_scope("activate"):
         preact = partials[0]
@@ -293,6 +288,7 @@
         even = lax.axis_index("layer") % 2 == 0
         far = passed_along(own, 2)
         late_far = passed_along(late_own, 2)
+        far, late_own = lax.optimization_barrier((far, late_own))
         near = across_cores(jnp.where(even, own, far))
     with jax.named_scope("decode"):
         groups = lax.bitwise_xor(place, jnp.array(held, jnp.int32))

time: 113 us -> 82.3 us (0.73); the launches traced: 113 us -> 80.8 us
  Pallas kernels: 43.7 us -> 12 us
  waiting for transfers between devices: 32.8 us -> 29.9 us
  other arithmetic: 3.93 us -> 5.09 us
    pallas_call x1, Pallas kernels: 32.9 us -> 1.02 us  [fetch_rows(): pl.pallas_call(fetch_rows_kernel, out_shape=[jax.ShapeDtypeStruct((depth,...]
    ppermute x4, waiting for transfers between devices: 9.89 us -> 0.01 us  [passed_along(): lax.ppermute(value, 'layer', [(i, i + steps) for i in range(count - steps)])]
    ppermute x8, waiting for transfers between devices: 21.7 us -> 27.4 us  [swapped(): return lax.ppermute(value, 'latent', [(i, i ^ step) for i in range(count)])]
    unnamed x18 -> x20, local copies, waits for them, and re-layouts: 2.93 us -> 4.51 us
    ppermute x2, waiting for transfers between devices: 1.16 us -> 2.47 us  [across_cores(): return lax.ppermute(value, 'layer', [(i, i ^ 1) for i in range(count)])]
    ppermute x4, starting transfers between devices: 11.5 us -> 12.8 us  [passed_along(): lax.ppermute(value, 'layer', [(i, i + steps) for i in range(count - steps)])]
  transfers between devices with their start and end apart: 14 -> 14, of which waited for: 6 -> 6; matrix products, arithmetic and copies ran while one was open for 7% -> 10% of each run, Pallas kernels for 6% -> 10%
where the time goes in v1:
time: 82.3 us; the launch traced here: 80.8 us
  waiting for transfers between devices  29.9 us (36%)
  starting transfers between devices  26.5 us (32%)
  Pallas kernels  12 us (15%)
  local copies, waits for them, and re-layouts  7.19 us (9%)
  other arithmetic  5.09 us (6%)
    ppermute x8, waiting for transfers between devices, swapped(): return lax.ppermute(value, 'latent', [(i, i ^ step) for i in range(count)])  27.4 us
    ppermute x4, starting transfers between devices, passed_along(): lax.ppermute(value, 'layer', [(i, i + steps) for i in range(count - steps)])  12.8 us
    ppermute x8, starting transfers between devices, swapped(): return lax.ppermute(value, 'latent', [(i, i ^ step) for i in range(count)])  10.9 us
    pallas_call x1, Pallas kernels, decode_early(): pl.pallas_call(early_kernel, out_shape=[jax.ShapeDtypeStruct((tokens, fea...  4.58 us
    unnamed x20, local copies, waits for them, and re-layouts  4.51 us
    pallas_call x1, Pallas kernels, decode_late(): pl.pallas_call(late_kernel, out_shape=jax.ShapeDtypeStruct((tokens, featu...  3.25 us
    pallas_call x1, Pallas kernels, encode(): pl.pallas_call(functools.partial(encode_kernel, parts), out_shape=[jax.Sh...  3.2 us
    ppermute x2, starting transfers between devices, across_cores(): return lax.ppermute(value, 'layer', [(i, i ^ 1) for i in range(count)])  2.79 us
  transfers between devices with their start and end apart: 14, of which 6 were waited for; matrix products, arithmetic and copies ran while one was open for 10% of the time, Pallas kernels for 10%

profile of v1, /device:TPU:5, one launch (start us, length us, event | category | flops | bytes accessed | tf_op | source)
XLA Modules:
  0.0 80.8 jit_solution(4412016244593222038)
XLA Ops:
  0.0 1.2 %copy-done.1 = bf16[1,4096,128]{2,1,0:T(8,128)(2,1)S(1)} copy-done((bf16[1,4096,128]{2,1,0:T(8,128)(2,1)S(1)}, bf16[1,4096,128]{2,1,0:T(8,128)(2,1)}, u32[]{:S(2)}) %copy-start.1) | copy-done | bytes 1048600
  1.2 1.0 %fetch_rows.1 = (bf16[1024,128]{1,0:T(8,128)(2,1)S(1)}, bf16[1024,128]{1,0:T(8,128)(2,1)}, bf16[1024,128]{1,0:T(8,128)(2,1)}, bf16[1024,128]{1,0:T(8,128)(2,1)}) custom-call(s32[1]{0:T(128)} %bitcast.place_ref, bf16[4096,128]{1,0:T(8,128)(2,1)S(1)} %bitcast.19), custom_call_target="tpu_custom_call" | custom-call | tf_op jit(solution)/shard_map/encoder_rows/fetch_rows/pallas_call | solution.py:55
  2.3 1.4 %collective-permute-start.2 = (bf16[1024,128]{1,0:T(8,128)(2,1)}, bf16[1024,128]{1,0:T(8,128)(2,1)}, u32[]{:S(2)}, u32[]{:S(2)}) collective-permute-start(bf16[1024,128]{1,0:T(8,128)(2,1)} %get-tuple-element.35), channel_id=1, source_target_pairs={{0,1},{1,0},{2,3},{3,2},{4,5},{5,4},{6,7},{7,6},{8,9},{9,8},{10,11... | collective-permute-start | bytes 786440 | tf_op jit(solution)/shard_map/encoder_rows/ppermute | solution.py:18
  3.6 2.3 %collective-permute-start.3 = (bf16[1024,128]{1,0:T(8,128)(2,1)}, bf16[1024,128]{1,0:T(8,128)(2,1)}, u32[]{:S(2)}, u32[]{:S(2)}) collective-permute-start(bf16[1024,128]{1,0:T(8,128)(2,1)} %get-tuple-element.36), channel_id=1, source_target_pairs={{0,2},{1,3},{2,0},{3,1},{4,6},{5,7},{6,4},{7,5},{8,10},{9,11},{10,... | collective-permute-start | bytes 786440 | tf_op jit(solution)/shard_map/encoder_rows/ppermute | solution.py:18
  5.9 0.0 collective-permute-start.4
  5.9 0.8 xor_bitcast_fusion
  6.7 0.1 copy.22
  6.8 2.2 %slice_bitcast_fusion = (bf16[512,1024]{1,0:T(8,128)(2,1)S(1)}, bf16[512,1024]{1,0:T(8,128)(2,1)S(1)}, bf16[512,1024]{1,0:T(8,128)(2,1)S(1)}) fusion(bf16[3,512,1024]{2,1,0:T(8,128)(2,1)} %bitcast.21), kind=kLoop, calls=%fused_computation.4 | loop fusion | bytes 6291456 | tf_op jit(solution)/shard_map/decoder_weights/squeeze | solution.py:266
  9.0 0.0 copy-start.5
  9.0 1.6 %fusion.1 = (bf16[528,1024]{1,0:T(8,128)(2,1)}, bf16[528,1024]{1,0:T(8,128)(2,1)}) fusion(bf16[16,2]{1,0:T(8,128)(2,1)S(1)} %copy.22, bf16[512,1024]{1,0:T(8,128)(2,1)S(1)} %get-tuple-element.55, bf16[512,1024]{1,0:T(8,128)(2,1)S(1)} %get-tuple-element.54), kind=kLoop, calls=%fused_computation.2 | loop fusion | flops 4866048 | bytes 4259904 | tf_op jit(solution)/shard_map/decoder_weights/concatenate | solution.py:69
  10.5 4.5 %collective-permute-start = (bf16[528,1024]{1,0:T(8,128)(2,1)}, bf16[528,1024]{1,0:T(8,128)(2,1)S(1)}, u32[]{:S(2)}, u32[]{:S(2)}) collective-permute-start(bf16[528,1024]{1,0:T(8,128)(2,1)} %get-tuple-element.56), channel_id=1, source_target_pairs={{0,4},{4,8},{8,12},{12,16},{16,20},{20,24},{24,28},{1,5},{5,9},{9,... | collective-permute-start | bytes 3244040 | tf_op jit(solution)/shard_map/decoder_weights/ppermute | solution.py:23
  15.0 1.9 %collective-permute-start.1 = (bf16[528,1024]{1,0:T(8,128)(2,1)}, bf16[528,1024]{1,0:T(8,128)(2,1)S(1)}, u32[]{:S(2)}, u32[]{:S(2)}) collective-permute-start(bf16[528,1024]{1,0:T(8,128)(2,1)} %get-tuple-element.57), channel_id=1, source_target_pairs={{0,8},{4,12},{8,16},{12,20},{16,24},{20,28},{1,9},{5,13},{9,17},{1... | collective-permute-start | bytes 3244040 | tf_op jit(solution)/shard_map/decoder_weights/ppermute | solution.py:23
  17.0 0.1 dynamic-slice_bitcast_fusion
  17.0 0.1 copy.25.relative_ref
  17.1 0.0 collective-permute-done.2.refs_1_
  17.1 6.0 %collective-permute-done.4.refs_3_ = bf16[1024,128]{1,0:T(8,128)(2,1)} collective-permute-done((bf16[1024,128]{1,0:T(8,128)(2,1)}, bf16[1024,128]{1,0:T(8,128)(2,1)}, u32[]{:S(2)}, u32[]{:S(2)}) %collective-permute-start.4) | collective-permute-done | bytes 262176 | tf_op jit(solution)/shard_map/encoder_rows/ppermute | solution.py:18
  23.1 1.6 %copy-done.4 = bf16[1,1024,1024]{2,1,0:T(8,128)(2,1)S(1)} copy-done((bf16[1,1024,1024]{2,1,0:T(8,128)(2,1)S(1)}, bf16[1,1024,1024]{2,1,0:T(8,128)(2,1)}, u32[]{:S(2)}) %copy-start.4) | copy-done | bytes 2097176
  24.7 3.2 %encode.1 = (f32[4,2,64,128]{3,2,1,0:T(8,128)S(1)}, bf16[4,2,64,128]{3,2,1,0:T(8,128)(2,1)S(1)}, bf16[4,2,64,128]{3,2,1,0:T(8,128)(2,1)S(1)}, bf16[4,2,64,128]{3,2,1,0:T(8,128)(2,1)S(1)}) custom-call(s32[1]{0:T(128)} %bitcast.place_ref, s32[16,2]{1,0:T(8,128)S(1)} %copy.25.relative_ref, f32[1,128]{1,0:T(1,128)S(1)} %copy-done.5, ...), custom_call_target="tpu_custom_call" | custom-call | flops 1073741824 | bytes 3145728 | tf_op jit(solution)/shard_map/encode/encode/pallas_call | solution.py:106
  27.9 1.1 %collective-permute-start.5 = (bf16[4,2,64,128]{3,2,1,0:T(8,128)(2,1)S(1)}, bf16[4,2,64,128]{3,2,1,0:T(8,128)(2,1)S(1)}, u32[]{:S(2)}, u32[]{:S(2)}) collective-permute-start(bf16[4,2,64,128]{3,2,1,0:T(8,128)(2,1)S(1)} %get-tuple-element.39), channel_id=1, source_target_pairs={{0,3},{1,2},{2,1},{3,0},{4,7},{5,6},{6,5},{7,4},{8,11},{9,10},{10,... | collective-permute-start | bytes 393224 | tf_op jit(solution)/shard_map/encode/ppermute | solution.py:18
  29.1 5.9 %collective-permute-start.6 = (bf16[4,2,64,128]{3,2,1,0:T(8,128)(2,1)S(1)}, bf16[4,2,64,128]{3,2,1,0:T(8,128)(2,1)S(1)}, u32[]{:S(2)}, u32[]{:S(2)}) collective-permute-start(bf16[4,2,64,128]{3,2,1,0:T(8,128)(2,1)S(1)} %get-tuple-element.40), channel_id=1, source_target_pairs={{0,2},{1,3},{2,0},{3,1},{4,6},{5,7},{6,4},{7,5},{8,10},{9,11},{10,... | collective-permute-start | bytes 393224 | tf_op jit(solution)/shard_map/encode/ppermute | solution.py:18
  35.0 0.1 collective-permute-start.7
  35.1 0.1 fusion.3
  35.2 0.0 collective-permute-done.5
  35.2 9.7 %collective-permute-done.6 = bf16[4,2,64,128]{3,2,1,0:T(8,128)(2,1)S(1)} collective-permute-done((bf16[4,2,64,128]{3,2,1,0:T(8,128)(2,1)S(1)}, bf16[4,2,64,128]{3,2,1,0:T(8,128)(2,1)S(1)}, u32[]{:S(2)}, u32[]{:S(2)}) %collective-permute-start.6) | collective-permute-done | bytes 131104 | tf_op jit(solution)/shard_map/encode/ppermute | solution.py:18
  44.9 0.0 collective-permute-done.7
  44.9 0.1 multiply_convert_fusion
  45.0 0.1 collective-permute-start.8
  45.1 8.3 %collective-permute-done.8 = bf16[4,2,64,128]{3,2,1,0:T(8,128)(2,1)S(1)} collective-permute-done((bf16[4,2,64,128]{3,2,1,0:T(8,128)(2,1)S(1)}, bf16[4,2,64,128]{3,2,1,0:T(8,128)(2,1)S(1)}, u32[]{:S(2)}, u32[]{:S(2)}) %collective-permute-start.8) | collective-permute-done | bytes 131104 | tf_op jit(solution)/shard_map/spread/ppermute | solution.py:18
  53.4 0.7 pad_maximum_fusion.own_early
  54.1 0.0 collective-permute-start.10
  54.1 3.1 %collective-permute-start.9 = (bf16[8,2,64,128]{3,2,1,0:T(8,128)(2,1)}, bf16[8,2,64,128]{3,2,1,0:T(8,128)(2,1)}, u32[]{:S(2)}, u32[]{:S(2)}) collective-permute-start(bf16[8,2,64,128]{3,2,1,0:T(8,128)(2,1)} %pad_maximum_fusion.own_early), channel_id=1, source_target_pairs={{0,8},{4,12},{8,16},{12,20},{16,24},{20,28},{1,9},{5,13},{9,17},{1... | collective-permute-start | bytes 786440 | tf_op jit(solution)/shard_map/spread/ppermute | solution.py:23
  57.3 0.0 collective-permute-done.near_dec
  57.3 0.1 copy.23
  57.4 3.4 %collective-permute-done.10.own_late = bf16[8,2,64,128]{3,2,1,0:T(8,128)(2,1)S(1)} collective-permute-done((bf16[8,2,64,128]{3,2,1,0:T(8,128)(2,1)}, bf16[8,2,64,128]{3,2,1,0:T(8,128)(2,1)S(1)}, u32[]{:S(2)}, u32[]{:S(2)}) %collective-permute-start.10) | collective-permute-done | bytes 262176 | tf_op jit(solution)/shard_map/spread/ppermute | solution.py:18
  60.8 0.7 copy-done.2
  61.5 3.2 %collective-permute-start.12 = (bf16[8,2,64,128]{3,2,1,0:T(8,128)(2,1)}, bf16[8,2,64,128]{3,2,1,0:T(8,128)(2,1)S(1)}, u32[]{:S(2)}, u32[]{:S(2)}) collective-permute-start(bf16[8,2,64,128]{3,2,1,0:T(8,128)(2,1)} %copy-done.2), channel_id=1, source_target_pairs={{0,8},{4,12},{8,16},{12,20},{16,24},{20,28},{1,9},{5,13},{9,17},{1... | collective-permute-start | bytes 786440 | tf_op jit(solution)/shard_map/spread/ppermute | solution.py:23
  64.7 0.0 collective-permute-done.9.far
  64.7 1.8 %broadcast_select_fusion.1 = bf16[8,2,64,128]{3,2,1,0:T(8,128)(2,1)} fusion(bf16[8,2,64,128]{3,2,1,0:T(8,128)(2,1)} %collective-permute-done.9.far, pred[]{:T(512)S(6)} %eq.5, bf16[4,2,64,128]{3,2,1,0:T(8,128)(2,1)} %copy-done.7, bf16[4,2,64,128]{3,2,1,0:T(8,128)(2,1)} %copy-done.6), kind=kLoop, calls=%fused_computation.10 | loop fusion | flops 262144 | bytes 786433 | tf_op jit(solution)/shard_map/spread/jit(_where)/select_n | solution.py:292
  66.5 2.4 %collective-permute-start.11 = (bf16[8,2,64,128]{3,2,1,0:T(8,128)(2,1)}, bf16[8,2,64,128]{3,2,1,0:T(8,128)(2,1)}, u32[]{:S(2)}, u32[]{:S(2)}) collective-permute-start(bf16[8,2,64,128]{3,2,1,0:T(8,128)(2,1)} %broadcast_select_fusion.1), channel_id=1, source_target_pairs={{0,4},{4,0},{8,12},{12,8},{16,20},{20,16},{24,28},{28,24},{1,5},{5... | collective-permute-start | bytes 786440 | tf_op jit(solution)/shard_map/spread/ppermute | solution.py:28
  68.9 0.1 copy.24
  69.0 0.1 copy.27.lists_ref
  69.1 1.3 %collective-permute-done.11.near = bf16[8,2,64,128]{3,2,1,0:T(8,128)(2,1)} collective-permute-done((bf16[8,2,64,128]{3,2,1,0:T(8,128)(2,1)}, bf16[8,2,64,128]{3,2,1,0:T(8,128)(2,1)}, u32[]{:S(2)}, u32[]{:S(2)}) %collective-permute-start.11) | collective-permute-done | bytes 262176 | tf_op jit(solution)/shard_map/spread/ppermute | solution.py:28
  70.4 0.9 %copy-done.3 = bf16[8,2,64,128]{3,2,1,0:T(8,128)(2,1)S(1)} copy-done((bf16[8,2,64,128]{3,2,1,0:T(8,128)(2,1)S(1)}, bf16[8,2,64,128]{3,2,1,0:T(8,128)(2,1)}, u32[]{:S(2)}) %copy-start.3) | copy-done | bytes 262168
  71.3 4.6 %decode_early.1 = (bf16[1024,1024]{1,0:T(8,128)(2,1)}, f32[512,1024]{1,0:T(8,128)S(1)}) custom-call(s32[4]{0:T(128)S(1)} %broadcast_xor_fusion.groups_ref, s32[3,16,2]{2,1,0:T(8,128)S(1)} %copy.27.lists_ref, bf16[8,2,64,128]{3,2,1,0:T(8,128)(2,1)} %pad_maximum_fusion.own_early, bf16[8,2,64,128]{3,2,1,0:T(8,128)(2,1)S(1)} %copy-done.3, ...), custom_call_target="tpu_custom_call" | custom-call | flops 2147483648 | bytes 7340032 | tf_op jit(solution)/shard_map/decode/decode_early/pallas_call | solution.py:207
  75.9 0.0 collective-permute-done.12.far
  76.0 0.4 collective-permute-start.13
  76.4 1.2 %collective-permute-done.13.near = bf16[8,2,64,128]{3,2,1,0:T(8,128)(2,1)S(1)} collective-permute-done((bf16[8,2,64,128]{3,2,1,0:T(8,128)(2,1)S(1)}, bf16[8,2,64,128]{3,2,1,0:T(8,128)(2,1)S(1)}, u32[]{:S(2)}, u32[]{:S(2)}) %collective-permute-start.13) | collective-permute-done | bytes 262176 | tf_op jit(solution)/shard_map/decode/ppermute | solution.py:28
  77.6 3.2 %decode_late.1 = bf16[1024,1024]{1,0:T(8,128)(2,1)} custom-call(s32[4]{0:T(128)S(1)} %broadcast_xor_fusion.groups_ref, s32[3,16,2]{2,1,0:T(8,128)S(1)} %copy.27.lists_ref, f32[512,1024]{1,0:T(8,128)S(1)} %get-tuple-element.50.partial_ref, bf16[8,2,64,128]{3,2,1,0:T(8,128)(2,1)S(1)} %collective-permute-done.13.near, ...), custom_call_target="tpu_custom_call", output_to_operand_aliasing={{}: (7, {})} | custom-call | flops 1073741824 | bytes 6291456 | tf_op jit(solution)/shard_map/decode/decode_late/pallas_call | solution.py:229
  (22 shorter events, 0.1 us)
Async XLA Ops:
  0.0 17.0 %copy-start = (s32[1,16]{1,0:T(1,128)S(1)}, s32[1,16]{1,0:T(1,128)}, u32[]{:S(2)}) copy-start(s32[1,16]{1,0:T(1,128)} %param.12) | copy-start | bytes 196
  0.0 1.2 %copy-start.1 = (bf16[1,4096,128]{2,1,0:T(8,128)(2,1)S(1)}, bf16[1,4096,128]{2,1,0:T(8,128)(2,1)}, u32[]{:S(2)}) copy-start(bf16[1,4096,128]{2,1,0:T(8,128)(2,1)} %param.8) | copy-start | bytes 3145732
  2.3 14.8 %collective-permute-start.2 = (bf16[1024,128]{1,0:T(8,128)(2,1)}, bf16[1024,128]{1,0:T(8,128)(2,1)}, u32[]{:S(2)}, u32[]{:S(2)}) collective-permute-start(bf16[1024,128]{1,0:T(8,128)(2,1)} %get-tuple-element.35), channel_id=1, source_target_pairs={{0,1},{1,0},{2,3},{3,2},{4,5},{5,4},{6,7},{7,6},{8,9},{9,8},{10,11... | collective-permute-start | bytes 786440 | tf_op jit(solution)/shard_map/encoder_rows/ppermute | solution.py:18
  3.6 13.5 %collective-permute-start.3 = (bf16[1024,128]{1,0:T(8,128)(2,1)}, bf16[1024,128]{1,0:T(8,128)(2,1)}, u32[]{:S(2)}, u32[]{:S(2)}) collective-permute-start(bf16[1024,128]{1,0:T(8,128)(2,1)} %get-tuple-element.36), channel_id=1, source_target_pairs={{0,2},{1,3},{2,0},{3,1},{4,6},{5,7},{6,4},{7,5},{8,10},{9,11},{10,... | collective-permute-start | bytes 786440 | tf_op jit(solution)/shard_map/encoder_rows/ppermute | solution.py:18
  5.9 17.2 %collective-permute-start.4 = (bf16[1024,128]{1,0:T(8,128)(2,1)}, bf16[1024,128]{1,0:T(8,128)(2,1)}, u32[]{:S(2)}, u32[]{:S(2)}) collective-permute-start(bf16[1024,128]{1,0:T(8,128)(2,1)} %get-tuple-element.37), channel_id=1, source_target_pairs={{0,3},{1,2},{2,1},{3,0},{4,7},{5,6},{6,5},{7,4},{8,11},{9,10},{10,... | collective-permute-start | bytes 786440 | tf_op jit(solution)/shard_map/encoder_rows/ppermute | solution.py:18
  9.0 14.2 %copy-start.5 = (f32[1,128]{1,0:T(1,128)S(1)}, f32[1,128]{1,0:T(1,128)}, u32[]{:S(2)}) copy-start(f32[1,128]{1,0:T(1,128)} %bias_ref.1) | copy-start | bytes 1540
  10.5 46.7 %collective-permute-start = (bf16[528,1024]{1,0:T(8,128)(2,1)}, bf16[528,1024]{1,0:T(8,128)(2,1)S(1)}, u32[]{:S(2)}, u32[]{:S(2)}) collective-permute-start(bf16[528,1024]{1,0:T(8,128)(2,1)} %get-tuple-element.56), channel_id=1, source_target_pairs={{0,4},{4,8},{8,12},{12,16},{16,20},{20,24},{24,28},{1,5},{5,9},{9,... | collective-permute-start | bytes 3244040 | tf_op jit(solution)/shard_map/decoder_weights/ppermute | solution.py:23
  15.0 45.8 %collective-permute-start.1 = (bf16[528,1024]{1,0:T(8,128)(2,1)}, bf16[528,1024]{1,0:T(8,128)(2,1)S(1)}, u32[]{:S(2)}, u32[]{:S(2)}) collective-permute-start(bf16[528,1024]{1,0:T(8,128)(2,1)} %get-tuple-element.57), channel_id=1, source_target_pairs={{0,8},{4,12},{8,16},{12,20},{16,24},{20,28},{1,9},{5,13},{9,17},{1... | collective-permute-start | bytes 3244040 | tf_op jit(solution)/shard_map/decoder_weights/ppermute | solution.py:23
  23.1 1.6 %copy-start.4 = (bf16[1,1024,1024]{2,1,0:T(8,128)(2,1)S(1)}, bf16[1,1024,1024]{2,1,0:T(8,128)(2,1)}, u32[]{:S(2)}) copy-start(bf16[1,1024,1024]{2,1,0:T(8,128)(2,1)} %param.7) | copy-start | bytes 6291460
  24.7 32.5 %copy-start.9 = (s32[4]{0:T(128)S(1)}, s32[4]{0:T(128)}, u32[]{:S(2)}) copy-start(s32[4]{0:T(128)} %constant.34.clone) | copy-start | bytes 52
  24.7 44.2 %copy-start.8 = (s32[1,16,2]{1,2,0:T(2,128)S(1)}, s32[1,16,2]{1,2,0:T(2,128)}, u32[]{:S(2)}) copy-start(s32[1,16,2]{1,2,0:T(2,128)} %param.11) | copy-start | bytes 388
  27.9 7.2 %collective-permute-start.5 = (bf16[4,2,64,128]{3,2,1,0:T(8,128)(2,1)S(1)}, bf16[4,2,64,128]{3,2,1,0:T(8,128)(2,1)S(1)}, u32[]{:S(2)}, u32[]{:S(2)}) collective-permute-start(bf16[4,2,64,128]{3,2,1,0:T(8,128)(2,1)S(1)} %get-tuple-element.39), channel_id=1, source_target_pairs={{0,3},{1,2},{2,1},{3,0},{4,7},{5,6},{6,5},{7,4},{8,11},{9,10},{10,... | collective-permute-start | bytes 393224 | tf_op jit(solution)/shard_map/encode/ppermute | solution.py:18
  29.1 15.8 %collective-permute-start.6 = (bf16[4,2,64,128]{3,2,1,0:T(8,128)(2,1)S(1)}, bf16[4,2,64,128]{3,2,1,0:T(8,128)(2,1)S(1)}, u32[]{:S(2)}, u32[]{:S(2)}) collective-permute-start(bf16[4,2,64,128]{3,2,1,0:T(8,128)(2,1)S(1)} %get-tuple-element.40), channel_id=1, source_target_pairs={{0,2},{1,3},{2,0},{3,1},{4,6},{5,7},{6,4},{7,5},{8,10},{9,11},{10,... | collective-permute-start | bytes 393224 | tf_op jit(solution)/shard_map/encode/ppermute | solution.py:18
  35.0 9.9 %collective-permute-start.7 = (bf16[4,2,64,128]{3,2,1,0:T(8,128)(2,1)S(1)}, bf16[4,2,64,128]{3,2,1,0:T(8,128)(2,1)S(1)}, u32[]{:S(2)}, u32[]{:S(2)}) collective-permute-start(bf16[4,2,64,128]{3,2,1,0:T(8,128)(2,1)S(1)} %get-tuple-element.41), channel_id=1, source_target_pairs={{0,1},{1,0},{2,3},{3,2},{4,5},{5,4},{6,7},{7,6},{8,9},{9,8},{10,11... | collective-permute-start | bytes 393224 | tf_op jit(solution)/shard_map/encode/ppermute | solution.py:18
  45.0 9.1 %copy-start.6 = (bf16[4,2,64,128]{3,2,1,0:T(8,128)(2,1)}, bf16[4,2,64,128]{3,2,1,0:T(8,128)(2,1)S(1)}, u32[]{:S(2)}) copy-start(bf16[4,2,64,128]{3,2,1,0:T(8,128)(2,1)S(1)} %multiply_convert_fusion) | copy-start | bytes 393220
  45.0 8.3 %collective-permute-start.8 = (bf16[4,2,64,128]{3,2,1,0:T(8,128)(2,1)S(1)}, bf16[4,2,64,128]{3,2,1,0:T(8,128)(2,1)S(1)}, u32[]{:S(2)}, u32[]{:S(2)}) collective-permute-start(bf16[4,2,64,128]{3,2,1,0:T(8,128)(2,1)S(1)} %multiply_convert_fusion), channel_id=1, source_target_pairs={{0,2},{1,3},{2,0},{3,1},{4,6},{5,7},{6,4},{7,5},{8,10},{9,11},{10,... | collective-permute-start | bytes 393224 | tf_op jit(solution)/shard_map/spread/ppermute | solution.py:18
  53.4 3.9 %copy-start.7 = (bf16[4,2,64,128]{3,2,1,0:T(8,128)(2,1)}, bf16[4,2,64,128]{3,2,1,0:T(8,128)(2,1)S(1)}, u32[]{:S(2)}) copy-start(bf16[4,2,64,128]{3,2,1,0:T(8,128)(2,1)S(1)} %collective-permute-done.8) | copy-start | bytes 393220
  54.1 6.7 %collective-permute-start.10 = (bf16[8,2,64,128]{3,2,1,0:T(8,128)(2,1)}, bf16[8,2,64,128]{3,2,1,0:T(8,128)(2,1)S(1)}, u32[]{:S(2)}, u32[]{:S(2)}) collective-permute-start(bf16[8,2,64,128]{3,2,1,0:T(8,128)(2,1)} %pad_maximum_fusion.own_early), channel_id=1, source_target_pairs={{0,1},{1,0},{2,3},{3,2},{4,5},{5,4},{6,7},{7,6},{8,9},{9,8},{10,11... | collective-permute-start | bytes 786440 | tf_op jit(solution)/shard_map/spread/ppermute | solution.py:18
  54.1 10.6 %collective-permute-start.9 = (bf16[8,2,64,128]{3,2,1,0:T(8,128)(2,1)}, bf16[8,2,64,128]{3,2,1,0:T(8,128)(2,1)}, u32[]{:S(2)}, u32[]{:S(2)}) collective-permute-start(bf16[8,2,64,128]{3,2,1,0:T(8,128)(2,1)} %pad_maximum_fusion.own_early), channel_id=1, source_target_pairs={{0,8},{4,12},{8,16},{12,20},{16,24},{20,28},{1,9},{5,13},{9,17},{1... | collective-permute-start | bytes 786440 | tf_op jit(solution)/shard_map/spread/ppermute | solution.py:23
  60.8 0.7 copy-start.2
  61.5 14.5 %collective-permute-start.12 = (bf16[8,2,64,128]{3,2,1,0:T(8,128)(2,1)}, bf16[8,2,64,128]{3,2,1,0:T(8,128)(2,1)S(1)}, u32[]{:S(2)}, u32[]{:S(2)}) collective-permute-start(bf16[8,2,64,128]{3,2,1,0:T(8,128)(2,1)} %copy-done.2), channel_id=1, source_target_pairs={{0,8},{4,12},{8,16},{12,20},{16,24},{20,28},{1,9},{5,13},{9,17},{1... | collective-permute-start | bytes 786440 | tf_op jit(solution)/shard_map/spread/ppermute | solution.py:23
  66.5 3.9 %collective-permute-start.11 = (bf16[8,2,64,128]{3,2,1,0:T(8,128)(2,1)}, bf16[8,2,64,128]{3,2,1,0:T(8,128)(2,1)}, u32[]{:S(2)}, u32[]{:S(2)}) collective-permute-start(bf16[8,2,64,128]{3,2,1,0:T(8,128)(2,1)} %broadcast_select_fusion.1), channel_id=1, source_target_pairs={{0,4},{4,0},{8,12},{12,8},{16,20},{20,16},{24,28},{28,24},{1,5},{5... | collective-permute-start | bytes 786440 | tf_op jit(solution)/shard_map/spread/ppermute | solution.py:28
  70.4 0.9 %copy-start.3 = (bf16[8,2,64,128]{3,2,1,0:T(8,128)(2,1)S(1)}, bf16[8,2,64,128]{3,2,1,0:T(8,128)(2,1)}, u32[]{:S(2)}) copy-start(bf16[8,2,64,128]{3,2,1,0:T(8,128)(2,1)} %copy-done.2) | copy-start | bytes 786436
  76.0 1.6 %collective-permute-start.13 = (bf16[8,2,64,128]{3,2,1,0:T(8,128)(2,1)S(1)}, bf16[8,2,64,128]{3,2,1,0:T(8,128)(2,1)S(1)}, u32[]{:S(2)}, u32[]{:S(2)}) collective-permute-start(bf16[8,2,64,128]{3,2,1,0:T(8,128)(2,1)S(1)} %broadcast_select_fusion), channel_id=1, source_target_pairs={{0,4},{4,0},{8,12},{12,8},{16,20},{20,16},{24,28},{28,24},{1,5},{5... | collective-permute-start | bytes 786440 | tf_op jit(solution)/shard_map/decode/ppermute | solution.py:28
